TPU v7x, 32 devices: a whole 2x2x4 slice. The times are simulated.
32 devices in a mesh: depth: 4 (over y, core), row: 2 (over x), col: 4 (over z).
Axes of the slice: x: 2, y: 2, z: 4, core: 2. Of those that a mesh axis runs over, the one named last changes fastest.
Arguments:
- expression: bfloat16 [3072, 8192], P('depth', 'col'), as said below
- offsets: int32 [4], P('depth'), may hold values from 0 to 256
Outputs:
- margin: float32 [8192, 8192], P('row', 'col')
Inputs may be any that keep to these rules, and one draw needn't show every extreme that they name: `expression`: finite values.
All inputs are finite; a program needn't handle non-finite values.
Results may differ from a plain program's by a relative error of at most 0.0003.
Values may be sent and summed in bfloat16 or wider, within the bound.
A program may use at most 256 MiB of HBM per device.

v0:
```python
import jax
import jax.numpy as jnp
from jax import lax
from jax.sharding import PartitionSpec as P

G = 8192
CW_DEV = 512
POWER = 6


def spread(block, axis, source):
    block = jnp.where(lax.axis_index(axis) == source, block, jnp.zeros_like(block))
    return lax.psum(block, axis)


def adjacent(corr, row_ids, col_ids):
    ident = row_ids[:, None] == col_ids[None, :]
    return jnp.where(ident, 0.0, lax.integer_pow(jnp.abs(corr), POWER))


def on_device(expression, offsets):
    n_row = lax.axis_size("row")
    n_col = lax.axis_size("col")
    n_depth = lax.axis_size("depth")
    depth_id = lax.axis_index("depth")
    tile_cols = expression.shape[1]
    tile_rows = G // n_row
    share = tile_rows // n_depth
    ratio = n_col // n_row
    cells_all = CW_DEV * n_depth
    window = lax.dynamic_slice_in_dim(expression, offsets[0], CW_DEV, 0)
    values = window.astype(jnp.float32)
    mean = lax.psum(jnp.sum(values, axis=0), "depth") / cells_all
    centred = values - mean
    variance = lax.psum(jnp.sum(centred * centred, axis=0), "depth") / cells_all
    scaled = (centred * lax.rsqrt(cells_all * (variance + 1e-05))).astype(jnp.bfloat16)
    pieces = []
    for part_index in range(ratio):
        pieces.append(spread(scaled, "col", lax.axis_index("row") * ratio + part_index))
    row_panel = jnp.concatenate(pieces, axis=1) if ratio > 1 else pieces[0]
    partial_corr = lax.dot_general(
        row_panel, scaled, (((0,), (0,)), ((), ())), preferred_element_type=jnp.float32
    )
    row_base = lax.axis_index("row") * tile_rows
    col_ids = lax.axis_index("col") * tile_cols + jnp.arange(tile_cols)
    corr_rows = lax.psum_scatter(partial_corr, "depth", scatter_dimension=0, tiled=True)
    corr = lax.all_gather(corr_rows, "depth", axis=0, tiled=True)
    a_full = adjacent(corr, row_base + jnp.arange(tile_rows), col_ids)
    a_half = a_full.astype(jnp.bfloat16)
    a_share = lax.dynamic_slice_in_dim(a_full, depth_id * share, share, 0)
    k_full = lax.psum(jnp.sum(a_full, axis=1), "col")
    k_rows = lax.dynamic_slice_in_dim(k_full, depth_id * share, share, 0)
    k_cols = lax.psum(jnp.sum(a_full, axis=0), "row")
    per_depth = n_col // n_depth
    lefts = []
    rights = []
    for step in range(per_depth):
        block = depth_id * per_depth + step
        lefts.append(spread(a_half, "col", block))
        upper = spread(a_half, "row", block // ratio)
        rights.append(lax.dynamic_slice_in_dim(upper, block % ratio * tile_cols, tile_cols, 0))
    total = jnp.zeros((share * lax.axis_size("depth"), tile_cols), jnp.float32)
    for step in range(per_depth):
        left_rows = lax.slice_in_dim(lefts[step], 0, share * lax.axis_size("depth"), axis=0)
        total = total + jnp.dot(left_rows, rights[step], preferred_element_type=jnp.float32)
    shared = lax.psum_scatter(total, "depth", scatter_dimension=0, tiled=True)
    share_ids = row_base + depth_id * share + jnp.arange(share)
    denom = jnp.minimum(k_rows[:, None], k_cols[None, :]) + 1.0 - a_share
    result = (shared + a_share) / denom
    result = jnp.where(share_ids[:, None] == col_ids[None, :], 1.0, result)
    return lax.all_gather(result, "depth", axis=0, tiled=True)


def solution(mesh):
    return jax.shard_map(
        on_device,
        mesh=mesh,
        in_specs=(P("depth", "col"), P("depth")),
        out_specs=P("row", "col"),
        check_vma=False,
    )
```

profile of v0, /device:TPU:0, one launch (start us, length us, event | category | flops | bytes accessed | tf_op | source)
XLA Modules:
  0.0 2141.3 jit_solution(10309424894379725312)
XLA Ops:
  7.3 2.3 convert_reduce_fusion
  9.7 8.5 psum.56
  18.2 2.4 fusion.5
  20.7 5.9 psum.57
  26.6 4.9 broadcast_select_fusion.3
  31.5 155.8 %all-reduce.9.cloned.1.call-done = (bf16[512,2048]{1,0:T(8,128)(2,1)}, bf16[512,2048]{1,0:T(8,128)(2,1)}) async-done(((bf16[512,2048]{1,0:T(8,128)(2,1)}, bf16[512,2048]{1,0:T(8,128)(2,1)}), (bf16[512,2048]{1,0:T(8,128)(2,1)}, bf16[512,2048]{1,0:T(8,128)(2,1)})) %all-reduce.9.cloned.1.call-update) | async-done | bytes 4194320 | tf_op jit(solution)/shard_map/psum | solution.py:13
  187.3 18.6 fusion.7
  205.9 234.0 %reduce-scatter.3.cloned.1.call-done = f32[1024,2048]{1,0:T(8,128)} async-done(((f32[4096,2048]{1,0:T(8,128)}), f32[1024,2048]{1,0:T(8,128)}) %reduce-scatter.3.cloned.1.call-update) | async-done | bytes 8388624 | tf_op jit(solution)/shard_map/reduce_scatter | solution.py:46
  440.0 203.1 %all-gather.3.cloned.1.call-done = f32[4096,2048]{1,0:T(8,128)} async-done(((f32[1024,2048]{1,0:T(8,128)}), f32[4096,2048]{1,0:T(8,128)}) %all-gather.3.cloned.1.call-update) | async-done | bytes 33554448 | tf_op jit(solution)/shard_map/all_gather | solution.py:47
  643.1 15.4 fusion.15
  658.6 13.6 broadcast_select_fusion
  672.1 7.6 copy-done
  679.8 0.5 all-reduce.5.cloned.1.call-update
  680.3 0.2 reduce-scatter.5.cloned.1.call-start
  680.6 377.3 %all-reduce.7.cloned.1.call-done = bf16[4096,2048]{1,0:T(8,128)(2,1)} async-done(((bf16[4096,2048]{1,0:T(8,128)(2,1)}), bf16[4096,2048]{1,0:T(8,128)(2,1)}) %all-reduce.7.cloned.1.call-update) | async-done | bytes 16777232 | tf_op jit(solution)/shard_map/psum | solution.py:13
  1057.9 564.9 %all-reduce.5.cloned.1.call-done = bf16[4096,2048]{1,0:T(8,128)(2,1)} async-done(((bf16[4096,2048]{1,0:T(8,128)(2,1)}), bf16[4096,2048]{1,0:T(8,128)(2,1)}) %all-reduce.5.cloned.1.call-update) | async-done | bytes 16777232 | tf_op jit(solution)/shard_map/psum | solution.py:13
  1622.8 43.3 %fusion.1 = f32[4096,2048]{1,0:T(8,128)} fusion(bf16[4096,2048]{1,0:T(8,128)(2,1)} %all-reduce.5.cloned.1.call-done, bf16[4096,2048]{1,0:T(8,128)(2,1)} %all-reduce.7.cloned.1.call-done, s32[]{:T(128)S(6)} %select_n.69), kind=kOutput, calls=%fused_computation.5 | convolution fusion | flops 34359738368 | bytes 58720260 | tf_op jit(solution)/shard_map/dot_general | solution.py:65
  1666.1 0.0 all-gather.5.cloned.1.call-start
  1666.2 16.1 psum.62
  1682.3 5.0 psum.63
  1687.3 212.8 %reduce-scatter.5.cloned.1.call-done = f32[1024,2048]{1,0:T(8,128)} async-done(((f32[4096,2048]{1,0:T(8,128)}), f32[1024,2048]{1,0:T(8,128)}) %reduce-scatter.5.cloned.1.call-update) | async-done | bytes 8388624 | tf_op jit(solution)/shard_map/reduce_scatter | solution.py:66
  1900.1 9.5 divide_select_fusion
  1909.6 201.7 %all-gather.5.cloned.1.call-done = f32[4096,2048]{1,0:T(8,128)} async-done(((f32[1024,2048]{1,0:T(8,128)}), f32[4096,2048]{1,0:T(8,128)}) %all-gather.5.cloned.1.call-update) | async-done | bytes 33554448 | tf_op jit(solution)/shard_map/all_gather | solution.py:71
  2111.3 23.2 %copy.9 = f32[4096,2048]{1,0:T(8,128)} copy(f32[4096,2048]{1,0:T(8,128)} %all-gather.5.cloned.1.call-done) | data formatting | bytes 67108864
  (20 shorter events, 0.3 us)
Async XLA Ops:
  6.5 180.8 %copy-start.1 = (bf16[768,2048]{1,0:T(8,128)(2,1)S(1)}, bf16[768,2048]{1,0:T(8,128)(2,1)}, u32[]{:S(2)}) copy-start(bf16[768,2048]{1,0:T(8,128)(2,1)} %param.2) | copy-start | bytes 9437188
  6.5 180.8 %all-reduce.9.cloned.1.call-start = ((), (), s32[]{:S(2)}) async-start(), calls=%async_computation.8 | async-start | bytes 8388608 | tf_op jit(solution)/shard_map/psum | solution.py:13
  31.5 408.4 %reduce-scatter.3.cloned.1.call-start = ((), (), s32[]{:S(2)}) async-start(), calls=%async_computation.2 | async-start | bytes 41943040 | tf_op jit(solution)/shard_map/reduce_scatter | solution.py:46
  205.9 437.2 %all-gather.3.cloned.1.call-start = ((), (), s32[]{:S(2)}) async-start(), calls=%async_computation.3 | async-start | bytes 41943040 | tf_op jit(solution)/shard_map/all_gather | solution.py:47
  439.9 617.9 %all-reduce.7.cloned.1.call-start = ((), (), s32[]{:S(2)}) async-start(), calls=%async_computation.5 | async-start | bytes 33554432 | tf_op jit(solution)/shard_map/psum | solution.py:13
  658.6 21.2 copy-start
  679.7 943.1 %all-reduce.5.cloned.1.call-start = ((), (), s32[]{:S(2)}) async-start(), calls=%async_computation.4 | async-start | bytes 33554432 | tf_op jit(solution)/shard_map/psum | solution.py:13
  680.3 1219.8 %reduce-scatter.5.cloned.1.call-start = ((), (), s32[]{:S(2)}) async-start(), calls=%async_computation.6 | async-start | bytes 41943040 | tf_op jit(solution)/shard_map/reduce_scatter | solution.py:66
  1666.1 445.1 %all-gather.5.cloned.1.call-start = ((), (), s32[]{:S(2)}) async-start(), calls=%async_computation.7 | async-start | bytes 41943040 | tf_op jit(solution)/shard_map/all_gather | solution.py:71
Sparse Core Ops, SparseCore 0:
  31.6 155.6 all-reduce.8
  206.0 233.8 reduce-scatter.2
  441.6 201.5 all-gather.2
  679.8 377.9 all-reduce.6
  1060.2 562.5 all-reduce.4
  1666.3 233.8 reduce-scatter.4
  1909.7 201.5 all-gather.4
where the time goes:
time: 2140 us
  waiting for transfers between devices  1950 us (91%)
  matrix products  61.9 us (3%)
  other arithmetic  48.2 us (2%)
  blocking collectives  35.5 us (2%)
  local copies, waits for them, and re-layouts  30.7 us (1%)
    psum x3, waiting for transfers between devices, spread(): return lax.psum(block, axis)  1100 us
    reduce_scatter x1, waiting for transfers between devices, on_device(): lax.psum_scatter(partial_corr, 'depth', scatter_dimension=0, tiled=True)  234 us
    reduce_scatter x1, waiting for transfers between devices, on_device(): shared = lax.psum_scatter(total, 'depth', scatter_dimension=0, tiled=True)  213 us
    all_gather x1, waiting for transfers between devices, on_device(): corr = lax.all_gather(corr_rows, 'depth', axis=0, tiled=True)  203 us
    all_gather x1, waiting for transfers between devices, on_device(): return lax.all_gather(result, 'depth', axis=0, tiled=True)  202 us
    dot_general x1, matrix products, on_device(): jnp.dot(left_rows, rights[step], preferred_element_type=jnp.float32)  43.3 us
  transfers between devices with their start and end apart: 7, of which 7 were waited for; matrix products, arithmetic and copies ran while one was open for 0% of the time, Pallas kernels for 0%

commit v1 on v0

v1 whole, which is shorter than its diff:
```python
import functools

import jax
import jax.numpy as jnp
from jax import lax
from jax.experimental import pallas as pl
from jax.experimental.pallas import tpu as pltpu
from jax.sharding import PartitionSpec as P

CW_DEV = 512
VMEM = 56 * 1024 * 1024
CHUNK = 256


def panel_kernel(rows_ref, x_ref, y_ref, *outs, n_cells, width, tiles):
    if tiles:
        half_ref, degree_ref, tile_ref = outs
    else:
        half_ref, degree_ref = outs
    i, j = pl.program_id(0), pl.program_id(1)
    block = half_ref.shape[0]
    shift = (j - (rows_ref[0] + i)) * block
    chunk = min(CHUNK, block)
    inside = (j >= rows_ref[1]) & (j < rows_ref[1] + width)
    partial = jnp.zeros((block, 128), jnp.float32)
    for start in range(0, block, chunk):
        corr = jnp.zeros((block, chunk), jnp.float32)
        for d in range(n_cells):
            corr = corr + lax.dot_general(
                x_ref[0, d, 0],
                y_ref[0, d, 0, start:start + chunk],
                (((1,), (1,)), ((), ())),
                preferred_element_type=jnp.float32,
            )
        square = corr * corr
        value = square * square * square
        gap = lax.broadcasted_iota(jnp.int32, value.shape, 0) - lax.broadcasted_iota(
            jnp.int32, value.shape, 1
        )
        value = jnp.where(gap == shift + start, 0.0, value)
        half_ref[:, start:start + chunk] = value.astype(jnp.bfloat16)
        for lane in range(0, chunk, 128):
            partial = partial + value[:, lane:lane + 128]
        if tiles:
            @pl.when(inside)
            def _(value=value, start=start):
                tile_ref[:, start:start + chunk] = value

    @pl.when(j == 0)
    def _():
        degree_ref[...] = partial

    @pl.when(j > 0)
    def _():
        degree_ref[...] += partial


def panel(cells, first, col_first, rows, width, block, genes, with_tile):
    n_row, n_cells, n_col, held, depth = cells.shape
    per_row = held // block
    per_col = per_row * n_row

    def place(g):
        rest = g % per_col
        return rest // per_row, 0, g // per_col, rest % per_row, 0

    n_i, n_j = rows // block, genes // block
    n_t = width // block
    shape = (1, n_cells, 1, block, depth)
    out_shape = [
        jax.ShapeDtypeStruct((rows, genes), jnp.bfloat16),
        jax.ShapeDtypeStruct((rows, 128), jnp.float32),
    ]
    out_specs = [
        pl.BlockSpec((block, block), lambda i, j, s: (i, j)),
        pl.BlockSpec((block, 128), lambda i, j, s: (i, 0)),
    ]
    if with_tile:
        out_shape.append(jax.ShapeDtypeStruct((rows, width), jnp.float32))
        out_specs.append(
            pl.BlockSpec(
                (block, block), lambda i, j, s: (i, jnp.clip(j - s[1], 0, n_t - 1))
            )
        )
    return pl.pallas_call(
        functools.partial(panel_kernel, n_cells=n_cells, width=n_t, tiles=with_tile),
        grid_spec=pltpu.PrefetchScalarGridSpec(
            num_scalar_prefetch=1,
            grid=(n_i, n_j),
            in_specs=[
                pl.BlockSpec(shape, lambda i, j, s: place(s[0] + i)),
                pl.BlockSpec(shape, lambda i, j, s: place(j)),
            ],
            out_specs=out_specs,
        ),
        out_shape=out_shape,
        compiler_params=pltpu.CompilerParams(vmem_limit_bytes=VMEM),
        cost_estimate=pl.CostEstimate(
            flops=2 * rows * genes * n_cells * depth,
            bytes_accessed=rows * genes * 2 + 2 * genes * n_cells * depth * n_i,
            transcendentals=0,
        ),
        name="adjacency_tiled" if with_tile else "adjacency",
    )(jnp.stack([first, col_first]).astype(jnp.int32), cells, cells)


def margin_kernel(s_ref, a_ref, b_ref, tile_ref, kr_ref, kc_ref, *rest):
    piece_ref, full_ref, total = rest[-3:]
    i, k = pl.program_id(0), pl.program_id(1)
    last = pl.num_programs(1) - 1
    rows, cols = piece_ref.shape
    part = lax.dot_general(
        a_ref[...], b_ref[...], (((1,), (1,)), ((), ())), preferred_element_type=jnp.float32
    )

    @pl.when(k == 0)
    def _():
        total[...] = part

    @pl.when((k > 0) & (k < last))
    def _():
        total[...] += part

    @pl.when(k == last)
    def _():
        adj = tile_ref[...]
        shared = total[...] + part
        denom = jnp.minimum(kr_ref[...], kc_ref[...]) + 1.0 - adj
        result = (shared + adj) / denom
        gap = lax.broadcasted_iota(jnp.int32, (rows, cols), 0) - lax.broadcasted_iota(
            jnp.int32, (rows, cols), 1
        )
        result = jnp.where(gap == s_ref[1] - i * rows, 1.0, result)
        piece_ref[...] = result
        full_ref[...] = result


def margin_piece(left, right, tile, k_rows, k_cols, index, pieces, core, gap, whole):
    rows, genes = left.shape
    cols = right.shape[0]
    size = rows // pieces
    step = min(1024, genes)
    in_specs = [
        pl.BlockSpec((size, step), lambda i, k, s: (index, k)),
        pl.BlockSpec((cols, step), lambda i, k, s: (0, k)),
        pl.BlockSpec((size, cols), lambda i, k, s: (index, 0)),
        pl.BlockSpec((size, 1), lambda i, k, s: (index, 0)),
        pl.BlockSpec((1, cols), lambda i, k, s: (0, 0)),
    ]
    args = [left, right, tile, k_rows, k_cols]
    aliases = {}
    if whole is not None:
        in_specs.append(pl.BlockSpec(memory_space=pl.ANY))
        args.append(whole)
        aliases = {6: 1}
    return pl.pallas_call(
        margin_kernel,
        grid_spec=pltpu.PrefetchScalarGridSpec(
            num_scalar_prefetch=1,
            grid=(1, genes // step),
            in_specs=in_specs,
            out_specs=[
                pl.BlockSpec((size, cols), lambda i, k, s: (0, 0)),
                pl.BlockSpec((size, cols), lambda i, k, s: (s[0], 0)),
            ],
            scratch_shapes=[pltpu.VMEM((size, cols), jnp.float32)],
        ),
        out_shape=[
            jax.ShapeDtypeStruct((size, cols), jnp.float32),
            jax.ShapeDtypeStruct((2 * rows, cols), jnp.float32),
        ],
        input_output_aliases=aliases,
        compiler_params=pltpu.CompilerParams(vmem_limit_bytes=VMEM),
        cost_estimate=pl.CostEstimate(
            flops=2 * size * genes * cols,
            bytes_accessed=2 * (size + cols) * genes + 12 * size * cols,
            transcendentals=0,
        ),
        name="margin",
    )(jnp.stack([core * pieces + index, gap - index * size]).astype(jnp.int32), *args)


def on_device(expression, offsets):
    n_row = lax.axis_size("row")
    n_col = lax.axis_size("col")
    n_depth = lax.axis_size("depth")
    row_id, col_id = lax.axis_index("row"), lax.axis_index("col")
    core = lax.axis_index("depth") % 2
    tile_cols = expression.shape[1]
    genes = tile_cols * n_col
    tile_rows = genes // n_row
    rows = tile_rows // 2
    cells_all = CW_DEV * n_depth
    window = lax.dynamic_slice_in_dim(expression, offsets[0], CW_DEV, 0)
    values = window.astype(jnp.float32)
    mean = lax.psum(jnp.sum(values, axis=0), "depth") / cells_all
    centred = values - mean
    variance = lax.psum(jnp.sum(centred * centred, axis=0), "depth") / cells_all
    held = tile_cols // n_row
    scale = lax.rsqrt(cells_all * (variance + 1e-05))
    mine = lax.dynamic_slice_in_dim(centred, row_id * held, held, 1)
    scale = lax.dynamic_slice_in_dim(scale, row_id * held, held, 0)
    scaled = (mine * scale).astype(jnp.bfloat16).T
    cells = lax.all_gather(scaled, ("row", "depth", "col"))
    cells = cells.reshape(n_row, n_depth, n_col, held, CW_DEV)
    block = min(held, rows, 1024)
    row_base = row_id * tile_rows + core * rows
    col_base = col_id * tile_cols
    col_first = col_base // block
    left, deg_left, tile = panel(
        cells, row_base // block, col_first, rows, tile_cols, block, genes, True
    )
    right, deg_right = panel(
        cells, col_first, col_first, tile_cols, tile_cols, block, genes, False
    )
    k_rows = jnp.sum(deg_left, axis=1, keepdims=True)
    k_cols = jnp.sum(deg_right, axis=1)[None, :]
    pieces = 4
    size = rows // pieces
    swap = [(i, i ^ 1) for i in range(n_depth)]
    whole = None
    arrived = []
    for index in range(pieces):
        piece, whole = margin_piece(
            left, right, tile, k_rows, k_cols, index, pieces, core, col_base - row_base, whole
        )
        arrived.append(lax.ppermute(piece, "depth", swap))
    for index in range(pieces):
        start = (1 - core) * rows + index * size
        whole = lax.dynamic_update_slice_in_dim(whole, arrived[index], start, 0)
    return whole


def solution(mesh):
    return jax.shard_map(
        on_device,
        mesh=mesh,
        in_specs=(P("depth", "col"), P("depth")),
        out_specs=P("row", "col"),
        check_vma=False,
    )
```

time: 2140 us -> 694 us (0.32)
  waiting for transfers between devices: 1950 us -> 198 us
  Pallas kernels: 0 us -> 378 us
  matrix products: 61.9 us -> 0 us
  local copies, waits for them, and re-layouts: 30.7 us -> 64.1 us
  other arithmetic: 48.2 us -> 15.1 us
    psum x3 -> x0, waiting for transfers between devices: 1100 us -> none  [spread(): return lax.psum(block, axis)]
    reduce_scatter x2 -> x0, waiting for transfers between devices: 447 us -> none  [the longest x1 234 us: on_device(): lax.psum_scatter(partial_corr, 'depth', scatter_dimension=0, tiled=True)]
    pallas_call x0 -> x6, Pallas kernels: none -> 378 us  [the longest x2 245 us: panel(): pl.pallas_call(functools.partial(panel_kernel, n_cells=n_cells, width=n_t...]
    all_gather x2 -> x1, waiting for transfers between devices: 405 us -> 197 us  [on_device(): cells = lax.all_gather(scaled, ('row', 'depth', 'col'))]
    dot_general x2 -> x0, matrix products: 61.9 us -> none  [the longest x1 43.3 us: on_device(): jnp.dot(left_rows, rights[step], preferred_element_type=jnp.float32)]
    all_gather x0 -> x1, local copies, waits for them, and re-layouts: none -> 44 us  [on_device(): cells = lax.all_gather(scaled, ('row', 'depth', 'col'))]
    unnamed x5 -> x0, local copies, waits for them, and re-layouts: 30.7 us -> none
    select_n x3 -> x0, other arithmetic: 27.9 us -> none  [the longest x2 18.5 us: spread(): jnp.where(lax.axis_index(axis) == source, block, jnp.zeros_like(block))]
  transfers between devices with their start and end apart: 7 -> 5, of which waited for: 7 -> 1; matrix products, arithmetic and copies ran while one was open for 0% -> 2% of each run, Pallas kernels for 0% -> 15%
where the time goes in v1:
time: 694 us; the launch traced here: 685 us
  Pallas kernels  378 us (54%)
  waiting for transfers between devices  198 us (29%)
  local copies, waits for them, and re-layouts  64.1 us (9%)
  other arithmetic  15.1 us (2%)
  blocking collectives  14.4 us (2%)
  between operations  14.4 us (2%)
    pallas_call x2, Pallas kernels, panel(): pl.pallas_call(functools.partial(panel_kernel, n_cells=n_cells, width=n_t...  245 us
    all_gather x1, waiting for transfers between devices, on_device(): cells = lax.all_gather(scaled, ('row', 'depth', 'col'))  197 us
    pallas_call x4, Pallas kernels, margin_piece(): pl.pallas_call(margin_kernel, grid_spec=pltpu.PrefetchScalarGridSpec(num_...  134 us
    all_gather x1, local copies, waits for them, and re-layouts, on_device(): cells = lax.all_gather(scaled, ('row', 'depth', 'col'))  44 us
    dynamic_update_slice x4, local copies, waits for them, and re-layouts, on_device(): whole = lax.dynamic_update_slice_in_dim(whole, arrived[index], start, 0)  18.8 us
  transfers between devices with their start and end apart: 5, of which 1 were waited for; matrix products, arithmetic and copies ran while one was open for 2% of the time, Pallas kernels for 15%

profile of v1, /device:TPU:0, one launch (start us, length us, event | category | flops | bytes accessed | tf_op | source)
XLA Modules:
  0.0 684.8 jit_solution(8990130792467200699)
XLA Ops:
  7.2 2.2 convert_reduce_fusion
  9.4 8.5 %psum.14 = f32[2048]{0:T(1024)S(1)} all-reduce(f32[2048]{0:T(1024)S(1)} %convert_reduce_fusion), channel_id=1, replica_groups=mesh['depth'=4,'row'=2,'col'=4] {'depth'}, use_global_device_ids=true, to_apply=%region_1.2 | all-reduce | flops 2048 | bytes 16384 | tf_op jit(solution)/shard_map/psum | solution.py:196
  17.9 4.5 multiply_reduce_fusion
  22.4 5.8 psum.15
  28.2 2.8 fusion
  31.2 0.6 pad_add_fusion.1
  31.8 0.7 pad_add_fusion.4
  32.4 0.6 pad_add_fusion
  33.0 197.5 %all-gather.3.cloned.1.call-done = bf16[32768,512]{0,1:T(8,128)(2,1)} async-done(((bf16[1024,512]{0,1:T(8,128)(2,1)}), bf16[32768,512]{0,1:T(8,128)(2,1)}) %all-gather.3.cloned.1.call-update) | async-done | bytes 33554448 | tf_op jit(solution)/shard_map/all_gather | solution.py:204
  230.5 44.0 %copy.7 = bf16[32768,512]{1,0:T(8,128)(2,1)} copy(bf16[32768,512]{0,1:T(8,128)(2,1)} %all-gather.3.cloned.1.call-done) | data formatting | bytes 67108864 | tf_op jit(solution)/shard_map/all_gather | solution.py:204
  274.5 161.0 %adjacency_tiled.1 = (bf16[2048,8192]{1,0:T(8,128)(2,1)}, f32[2048,128]{1,0:T(8,128)}, f32[2048,2048]{1,0:T(8,128)}) custom-call(s32[2]{0:T(128)} %get-tuple-element.35.rows_ref, bf16[2,4,4,1024,512]{4,3,2,1,0:T(8,128)(2,1)} %bitcast.19, bf16[2,4,4,1024,512]{4,3,2,1,0:T(8,128)(2,1)} %bitcast.20), custom_call_target="tpu_custom_call" | custom-call | flops 68719476736 | bytes 100663296 | tf_op jit(solution)/shard_map/adjacency_tiled/pallas_call | solution.py:85
  435.5 1.6 reduce_sum.38
  437.1 1.4 copy.11.kr_ref
  438.5 83.5 %adjacency.1 = (bf16[2048,8192]{1,0:T(8,128)(2,1)}, f32[2048,128]{1,0:T(8,128)}) custom-call(s32[2]{0:T(128)} %get-tuple-element.36.rows_ref, bf16[2,4,4,1024,512]{4,3,2,1,0:T(8,128)(2,1)} %bitcast.21, bf16[2,4,4,1024,512]{4,3,2,1,0:T(8,128)(2,1)} %bitcast.22), custom_call_target="tpu_custom_call" | custom-call | flops 68719476736 | bytes 100663296 | tf_op jit(solution)/shard_map/adjacency/pallas_call | solution.py:85
  522.0 2.2 reduce_sum.39
  524.1 33.4 %margin.4 = (f32[512,2048]{1,0:T(8,128)}, f32[4096,2048]{1,0:T(8,128)}) custom-call(s32[2]{0:T(128)} %get-tuple-element.38.s_ref, bf16[2048,8192]{1,0:T(8,128)(2,1)} %get-tuple-element.18.a_ref, bf16[2048,8192]{1,0:T(8,128)(2,1)} %get-tuple-element.19.b_ref, f32[2048,2048]{1,0:T(8,128)} %get-tuple-element.20.tile_ref, f32[2048,1]{1,0:T(8,128)} %copy.11.kr_ref, ...), custom_call_target="tpu_custom_call" | custom-call | flops 17179869184 | bytes 54525952 | tf_op jit(solution)/shard_map/margin/pallas_call | solution.py:156
  557.8 33.7 %margin.5 = (f32[512,2048]{1,0:T(8,128)}, f32[4096,2048]{1,0:T(8,128)}) custom-call(s32[2]{0:T(128)} %get-tuple-element.37.s_ref, bf16[2048,8192]{1,0:T(8,128)(2,1)} %get-tuple-element.18.a_ref, bf16[2048,8192]{1,0:T(8,128)(2,1)} %get-tuple-element.19.b_ref, f32[2048,2048]{1,0:T(8,128)} %get-tuple-element.20.tile_ref, ...), custom_call_target="tpu_custom_call", output_to_operand_aliasing={{1}: (6, {})} | custom-call | flops 17179869184 | bytes 54525952 | tf_op jit(solution)/shard_map/margin/pallas_call | solution.py:156
  591.7 33.3 %margin.6 = (f32[512,2048]{1,0:T(8,128)}, f32[4096,2048]{1,0:T(8,128)}) custom-call(s32[2]{0:T(128)} %get-tuple-element.34.s_ref, bf16[2048,8192]{1,0:T(8,128)(2,1)} %get-tuple-element.18.a_ref, bf16[2048,8192]{1,0:T(8,128)(2,1)} %get-tuple-element.19.b_ref, f32[2048,2048]{1,0:T(8,128)} %get-tuple-element.20.tile_ref, ...), custom_call_target="tpu_custom_call", output_to_operand_aliasing={{1}: (6, {})} | custom-call | flops 17179869184 | bytes 54525952 | tf_op jit(solution)/shard_map/margin/pallas_call | solution.py:156
  625.0 0.3 collective-permute-start.2
  625.3 33.3 %margin.7 = (f32[512,2048]{1,0:T(8,128)}, f32[4096,2048]{1,0:T(8,128)}) custom-call(s32[2]{0:T(128)} %get-tuple-element.33.s_ref, bf16[2048,8192]{1,0:T(8,128)(2,1)} %get-tuple-element.18.a_ref, bf16[2048,8192]{1,0:T(8,128)(2,1)} %get-tuple-element.19.b_ref, f32[2048,2048]{1,0:T(8,128)} %get-tuple-element.20.tile_ref, ...), custom_call_target="tpu_custom_call", output_to_operand_aliasing={{1}: (6, {})} | custom-call | flops 17179869184 | bytes 54525952 | tf_op jit(solution)/shard_map/margin/pallas_call | solution.py:156
  658.9 4.7 constant_dynamic-update-slice_fusion.3
  663.6 4.7 constant_dynamic-update-slice_fusion.2
  668.3 4.7 constant_dynamic-update-slice_fusion.1
  673.0 4.7 constant_dynamic-update-slice_fusion
  (11 shorter events, 0.8 us)
Async XLA Ops:
  6.5 224.0 %all-gather.3.cloned.1.call-start = ((), (), s32[]{:S(2)}) async-start(), calls=%async_computation | async-start | bytes 34603008 | tf_op jit(solution)/shard_map/all_gather | solution.py:204
  557.6 101.3 %collective-permute-start = (f32[512,2048]{1,0:T(8,128)}, f32[512,2048]{1,0:T(8,128)}, u32[]{:S(2)}, u32[]{:S(2)}) collective-permute-start(f32[512,2048]{1,0:T(8,128)} %get-tuple-element.27), channel_id=1, source_target_pairs={{0,8},{8,0},{16,24},{24,16},{1,9},{9,1},{17,25},{25,17},{2,10},{10... | collective-permute-start | bytes 12582920 | tf_op jit(solution)/shard_map/ppermute | solution.py:227
  591.5 72.1 %collective-permute-start.1 = (f32[512,2048]{1,0:T(8,128)}, f32[512,2048]{1,0:T(8,128)}, u32[]{:S(2)}, u32[]{:S(2)}) collective-permute-start(f32[512,2048]{1,0:T(8,128)} %get-tuple-element.28), channel_id=1, source_target_pairs={{0,8},{8,0},{16,24},{24,16},{1,9},{9,1},{17,25},{25,17},{2,10},{10... | collective-permute-start | bytes 12582920 | tf_op jit(solution)/shard_map/ppermute | solution.py:227
  625.0 43.3 %collective-permute-start.2 = (f32[512,2048]{1,0:T(8,128)}, f32[512,2048]{1,0:T(8,128)}, u32[]{:S(2)}, u32[]{:S(2)}) collective-permute-start(f32[512,2048]{1,0:T(8,128)} %get-tuple-element.29), channel_id=1, source_target_pairs={{0,8},{8,0},{16,24},{24,16},{1,9},{9,1},{17,25},{25,17},{2,10},{10... | collective-permute-start | bytes 12582920 | tf_op jit(solution)/shard_map/ppermute | solution.py:227
  658.6 14.4 %collective-permute-start.3 = (f32[512,2048]{1,0:T(8,128)}, f32[512,2048]{1,0:T(8,128)}, u32[]{:S(2)}, u32[]{:S(2)}) collective-permute-start(f32[512,2048]{1,0:T(8,128)} %get-tuple-element.30), channel_id=1, source_target_pairs={{0,8},{8,0},{16,24},{24,16},{1,9},{9,1},{17,25},{25,17},{2,10},{10... | collective-permute-start | bytes 12582920 | tf_op jit(solution)/shard_map/ppermute | solution.py:227
Sparse Core Ops, SparseCore 0:
  31.2 199.2 all-gather.2
